TPU v7x, 32 devices: a whole 2x2x4 slice. The times are simulated.
32 devices in a mesh: parts: 1, ctx: 32 (over z, y, x, core).
Axes of the slice: x: 2, y: 2, z: 4, core: 2. Of those that a mesh axis runs over, the one named last changes fastest.
Arguments:
- q_lin: bfloat16 [2048, 4096], P(('parts', 'ctx')), may hold values from -6 to 6
- k_lin: bfloat16 [2048, 4096], P(('parts', 'ctx')), may hold values from -6 to 6
- v_lin: bfloat16 [2048, 4096], P(('parts', 'ctx')), may hold values from -6 to 6
- log_decay: float32 [2048, 32], P(('parts', 'ctx')), may hold values from -2 to 0
- pattern: int32 [64, 2], P(('parts', 'ctx')), may hold values 0 or 1
- q_soft: bfloat16 [2048, 4096], P(('parts', 'ctx')), may hold values from -64 to 64
- k_soft: bfloat16 [2048, 512], P(('parts', 'ctx')), may hold values from -4 to 4
- v_soft: bfloat16 [2048, 512], P(('parts', 'ctx')), may hold values from -6 to 6
Outputs:
- lightning_out: bfloat16 [2048, 4096], P(('parts', 'ctx'))
- softmax_out: bfloat16 [2048, 4096], P(('parts', 'ctx'))
All inputs are finite; a program needn't handle non-finite values. No bound on the sum of `pattern` on one device may be relied on, other than what follows from the above.
Results may differ from a plain program's by a relative error of at most 0.012.
Values may be sent and summed in bfloat16 or wider, within the bound.
A program may use at most 320 MiB of HBM per device.

v0:
```python
import math

import jax
import jax.numpy as jnp
from jax import lax
from jax.sharding import PartitionSpec as P

DH = 128
HQ = 32
KVH = 4


def entering(array, axis, combine, identity):
    peers, here = (lax.axis_size(axis), lax.axis_index(axis))
    everything = jax.tree.map(
        lambda part, kind: lax.all_gather(part.astype(kind), axis),
        array,
        (jnp.bfloat16, jnp.bfloat16),
    )
    start = jax.tree.map(
        lambda part, zero: jnp.broadcast_to(jnp.asarray(zero, part.dtype), part.shape),
        array,
        identity,
    )

    def step(k, before):
        reached = k < here
        new = combine(
            before, jax.tree.map(lambda part, own: part[k].astype(own.dtype), everything, array)
        )
        return jax.tree.map(lambda a, b: jnp.where(reached, a, b), new, before)

    return lax.fori_loop(0, peers, step, start)


def largest_divisor(count, limit):
    best = 1
    for cand in range(1, min(count, limit) + 1):
        if count % cand == 0:
            best = cand
    return best


def per_device(q_lin, k_lin, v_lin, log_decay, pattern, q_soft, k_soft, v_soft):
    tok = q_lin.shape[0]
    heads_lin = log_decay.shape[1]
    blocks = pattern.shape[1]
    queries = q_lin.reshape(tok, heads_lin, DH)
    keys = k_lin.reshape(tok, heads_lin, DH)
    values = v_lin.reshape(tok, heads_lin, DH)
    ell = jnp.cumsum(log_decay, axis=0)
    ell_end = ell[-1]
    decayed = (keys.astype(jnp.float32) * jnp.exp(ell_end[None, :] - ell)[:, :, None]).astype(
        jnp.bfloat16
    )
    summary = jnp.einsum("thd,the->hde", decayed, values, preferred_element_type=jnp.float32)

    def chain(earlier, later):
        return (earlier[0] * later[0], later[0][:, None, None] * earlier[1] + later[1])

    identity = (jnp.ones((heads_lin,), jnp.float32), jnp.zeros_like(summary))
    carried = entering((jnp.exp(ell_end), summary), "ctx", chain, identity)
    state_round = carried[1].astype(jnp.bfloat16)
    scores = jnp.einsum("thd,shd->hts", queries, keys, preferred_element_type=jnp.float32)
    index = jnp.arange(blocks)
    allowed = (pattern == 1) & (index[None, :] < index[:, None]) | (
        index[:, None] == index[None, :]
    )
    width = tok // blocks
    block_mask = jnp.broadcast_to(
        allowed[:, None, :, None], (blocks, width, blocks, width)
    ).reshape(tok, tok)
    position = jnp.arange(tok)
    live = block_mask & (position[None, :] <= position[:, None])
    ell_heads = ell.T
    diff = ell_heads[:, :, None] - ell_heads[:, None, :]
    decay = jnp.where(live[None], jnp.exp(jnp.where(live[None], diff, 0.0)), 0.0)
    lin_weights = (scores * decay).astype(jnp.bfloat16)
    intra = jnp.einsum("hts,she->the", lin_weights, values, preferred_element_type=jnp.float32)
    inter = (
        jnp.einsum("thd,hde->the", queries, state_round, preferred_element_type=jnp.float32)
        * jnp.exp(ell)[:, :, None]
    )
    mixed = inter + intra
    normed = mixed / jnp.sqrt(jnp.mean(mixed * mixed, axis=-1, keepdims=True) + 1e-06)
    lightning_out = normed.astype(jnp.bfloat16).reshape(tok, heads_lin * DH)
    group = HQ // KVH
    scale = 1.0 / math.sqrt(DH)
    grouped = q_soft.reshape(tok, KVH, group, DH)
    my_start = lax.axis_index("ctx") * tok
    my_last = my_start + tok - 1
    query_pos = my_start + jnp.arange(tok)

    def fold_block(carry, pairs, key_start):
        count = pairs.shape[1]
        block_keys = pairs[0].reshape(count, KVH, DH)
        block_values = pairs[1].reshape(count, KVH, DH)
        block_scores = (
            jnp.einsum("tkgd,skd->kgts", grouped, block_keys, preferred_element_type=jnp.float32)
            * scale
        )
        key_pos = key_start + jnp.arange(count)
        mask = (key_pos[None, :] <= query_pos[:, None]) & (key_pos[None, :] >= 0)
        running, total, accum = carry
        fresh = jnp.maximum(running, jnp.max(jnp.where(mask, block_scores, -1e30), axis=-1))
        probs = jnp.where(mask, jnp.exp(block_scores - fresh[..., None]), 0.0)
        factor = jnp.exp(running - fresh)
        total = total * factor + jnp.sum(probs, axis=-1)
        accum = accum * factor[..., None] + jnp.einsum(
            "kgts,skd->kgtd",
            probs.astype(jnp.bfloat16),
            block_values,
            preferred_element_type=jnp.float32,
        )
        return (fresh, total, accum)

    initial = (
        jnp.full((KVH, group, tok), -1e30, jnp.float32),
        jnp.zeros((KVH, group, tok), jnp.float32),
        jnp.zeros((KVH, group, tok, DH), jnp.float32),
    )
    own_pairs = jnp.stack([k_soft, v_soft])
    pairs = lax.all_gather(own_pairs, "ctx", axis=1, tiled=True)
    key_start = jnp.int32(0)
    count = pairs.shape[1]
    step = largest_divisor(count, 512)

    def loop_body(turn, state):
        piece = lax.dynamic_slice_in_dim(pairs, turn * step, step, 1)
        start = key_start + turn * step
        needed = (start <= my_last) & (start + step > 0)
        return lax.cond(
            needed, lambda inner: fold_block(inner, piece, start), lambda inner: inner, state
        )

    carry = lax.fori_loop(0, count // step, loop_body, initial)
    accum = carry[2] / carry[1][..., None]
    softmax_out = jnp.transpose(accum, (2, 0, 1, 3)).reshape(tok, HQ * DH).astype(jnp.bfloat16)
    return (lightning_out, softmax_out)


def solution(mesh):
    in_specs = (
        P(("parts", "ctx"), None),
        P(("parts", "ctx"), None),
        P(("parts", "ctx"), None),
        P(("parts", "ctx"), None),
        P(("parts", "ctx"), None),
        P(("parts", "ctx"), None),
        P(("parts", "ctx"), None),
        P(("parts", "ctx"), None),
    )
    out_specs = (P(("parts", "ctx"), None), P(("parts", "ctx"), None))
    return jax.shard_map(
        per_device, mesh=mesh, in_specs=in_specs, out_specs=out_specs, check_vma=False
    )
```

profile of v0, /device:TPU:31, one launch (start us, length us, event | category | flops | bytes accessed | tf_op | source)
XLA Modules:
  0.0 352.0 jit_solution(11650779153131371059)
XLA Ops:
  10.1 3.2 convolution_convert_fusion
  13.3 35.9 %all-gather.1 = bf16[32,1,32]{2,1,0:T(2,128)(2,1)S(1)} all-gather(bf16[1,1,32]{2,1,0:T(2,128)(2,1)S(1)} %get-tuple-element.409), channel_id=1, replica_groups=mesh['parts'=1,'ctx'=32] {'ctx'}, dimensions={0}, use_global_device_ids=true | all-gather | bytes 2112 | tf_op jit(solution)/shard_map/all_gather | solution.py:16
  49.9 22.6 %all-gather.5.cloned.1.call-done = bf16[2,2048,512]{2,0,1:T(2,128)(2,1)} async-done(((bf16[2,64,512]{2,0,1:T(2,128)(2,1)}), bf16[2,2048,512]{2,0,1:T(2,128)(2,1)}) %all-gather.5.cloned.1.call-update) | async-done | bytes 4194320 | tf_op jit(solution)/shard_map/all_gather | solution.py:123
  72.5 11.2 %copy.68 = bf16[2,2048,512]{1,2,0:T(8,128)(2,1)} copy(bf16[2,2048,512]{2,0,1:T(2,128)(2,1)} %all-gather.5.cloned.1.call-done) | data formatting | bytes 8388608
  84.8 23.6 %while.32 = (s32[]{:T(128)}, f32[4,8,64]{2,1,0:T(8,128)S(1)}, f32[4,8,64]{2,1,0:T(8,128)S(1)}, f32[4,8,64,128]{3,2,1,0:T(8,128)}, s32[]{:T(128)}, /*index=5*/bf1...) while((s32[]{:T(128)}, f32[4,8,64]{2,1,0:T(8,128)S(1)}, ...), condition=%wide.region_9.10_spmd.clone, body=%wide.region_4.9_spmd.clone.sunk | while | flops 549000768 | bytes 27007376 | solution.py:136
  84.8 6.0 %conditional.3 = ((f32[4,8,64]{2,1,0:T(8,128)S(1)}, f32[4,8,64]{2,1,0:T(8,128)S(1)}, f32[4,8,64,128]{3,2,1,0:T(8,128)})) conditional(s32[]{:T(128)} %convert_element_type.106, (f32[4,8,64]{2,1,0:T(8,128)S(1)}, f32[4,8,64]{2,1,0:T(8,128)S(1)}, f32[4,8,64,128]{3,2,1,0:T(8,128)}) %tuple.84, (s32[]{:T(128)}, s32[]{:T(128)}, ...), branch_computations={%region_5.5_spmd, %region_6.8_spmd} | conditional | flops 549000768 | bytes 27006874 | solution.py:132
  84.8 1.4 constant_dynamic-slice_fusion.1
  90.9 5.9 %conditional.3 = ((f32[4,8,64]{2,1,0:T(8,128)S(1)}, f32[4,8,64]{2,1,0:T(8,128)S(1)}, f32[4,8,64,128]{3,2,1,0:T(8,128)})) conditional(s32[]{:T(128)} %convert_element_type.106, (f32[4,8,64]{2,1,0:T(8,128)S(1)}, f32[4,8,64]{2,1,0:T(8,128)S(1)}, f32[4,8,64,128]{3,2,1,0:T(8,128)}) %tuple.84, (s32[]{:T(128)}, s32[]{:T(128)}, ...), branch_computations={%region_5.5_spmd, %region_6.8_spmd} | conditional | flops 549000768 | bytes 27006874 | solution.py:132
  96.7 5.9 %conditional.3 = ((f32[4,8,64]{2,1,0:T(8,128)S(1)}, f32[4,8,64]{2,1,0:T(8,128)S(1)}, f32[4,8,64,128]{3,2,1,0:T(8,128)})) conditional(s32[]{:T(128)} %convert_element_type.106, (f32[4,8,64]{2,1,0:T(8,128)S(1)}, f32[4,8,64]{2,1,0:T(8,128)S(1)}, f32[4,8,64,128]{3,2,1,0:T(8,128)}) %tuple.84, (s32[]{:T(128)}, s32[]{:T(128)}, ...), branch_computations={%region_5.5_spmd, %region_6.8_spmd} | conditional | flops 549000768 | bytes 27006874 | solution.py:132
  102.6 5.9 %conditional.3 = ((f32[4,8,64]{2,1,0:T(8,128)S(1)}, f32[4,8,64]{2,1,0:T(8,128)S(1)}, f32[4,8,64,128]{3,2,1,0:T(8,128)})) conditional(s32[]{:T(128)} %convert_element_type.106, (f32[4,8,64]{2,1,0:T(8,128)S(1)}, f32[4,8,64]{2,1,0:T(8,128)S(1)}, f32[4,8,64,128]{3,2,1,0:T(8,128)}) %tuple.84, (s32[]{:T(128)}, s32[]{:T(128)}, ...), branch_computations={%region_5.5_spmd, %region_6.8_spmd} | conditional | flops 549000768 | bytes 27006874 | solution.py:132
  106.1 1.4 fusion.13
  108.4 1.6 fusion.40
  111.4 156.8 %all-gather.7.cloned.1.call-done = bf16[1024,128,128]{2,1,0:T(8,128)(2,1)} async-done(((bf16[32,128,128]{2,1,0:T(8,128)(2,1)}), bf16[1024,128,128]{2,1,0:T(8,128)(2,1)}) %all-gather.7.cloned.1.call-update) | async-done | bytes 33554448 | tf_op jit(solution)/shard_map/all_gather | solution.py:16
  268.2 72.2 %while.33 = (s32[]{:T(128)}, f32[32,128,128]{2,1,0:T(8,128)S(1)}, s32[]{:T(128)}, bf16[32,32]{1,0:T(8,128)(2,1)S(1)}, bf16[32,32,128,128]{3,2,1,0:T(8,128)(2,1)}, /*index=5*/s32[]{:T(128)}, s32[]{:T(128)}) while((s32[]{:T(128)}, f32[32,128,128]{2,1,0:T(8,128)S(1)}, s32[]{:T(128)}, bf16[32,32]{1,0:T(8,128)(2,1)S(1)}, ...), condition=%wide.region_2.3_spmd.clone, body=%wide.region_1.2_spmd.clone.sunk | while | flops 2621476 | bytes 5243305 | solution.py:33
  268.2 2.3 fusion.68
  270.5 2.2 fusion.68
  272.8 2.2 fusion.68
  275.0 2.2 fusion.68
  277.3 2.2 fusion.68
  279.6 2.2 fusion.68
  281.8 2.2 fusion.68
  284.1 2.2 fusion.68
  286.3 2.2 fusion.68
  288.6 2.2 fusion.68
  290.8 2.2 fusion.68
  293.1 2.2 fusion.68
  295.3 2.2 fusion.68
  297.6 2.2 fusion.68
  299.9 2.2 fusion.68
  302.1 2.2 fusion.68
  304.4 2.2 fusion.68
  306.6 2.2 fusion.68
  308.9 2.2 fusion.68
  311.1 2.2 fusion.68
  313.4 2.2 fusion.68
  315.7 2.2 fusion.68
  317.9 2.2 fusion.68
  320.2 2.2 fusion.68
  322.4 2.2 fusion.68
  324.7 2.2 fusion.68
  326.9 2.2 fusion.68
  329.2 2.2 fusion.68
  331.5 2.2 fusion.68
  333.7 2.2 fusion.68
  336.0 2.2 fusion.68
  338.2 2.2 fusion.68
  340.5 1.4 fusion.20
  341.8 2.2 multiply_reduce_fusion
  (130 shorter events, 27.9 us)
Async XLA Ops:
  7.2 2.9 copy-start
  7.2 42.1 %copy-start.5 = (s32[2,2]{1,0:T(2,128)S(1)}, s32[2,2]{1,0:T(2,128)}, u32[]{:S(2)}) copy-start(s32[2,2]{1,0:T(2,128)} %param.18) | copy-start | bytes 52
  7.2 42.3 %copy-start.4 = (bf16[64,4096]{1,0:T(8,128)(2,1)S(1)}, bf16[64,4096]{1,0:T(8,128)(2,1)}, u32[]{:S(2)}) copy-start(bf16[64,4096]{1,0:T(8,128)(2,1)} %param.19) | copy-start | bytes 1572868
  7.2 65.3 %all-gather.5.cloned.1.call-start = ((), (), s32[]{:S(2)}) async-start(), calls=%async_computation | async-start | bytes 4325376 | tf_op jit(solution)/shard_map/all_gather | solution.py:123
  9.0 259.2 %all-gather.7.cloned.1.call-start = ((), (), s32[]{:S(2)}) async-start(), calls=%async_computation.1 | async-start | bytes 34603008 | tf_op jit(solution)/shard_map/all_gather | solution.py:16
  86.4 2.1 copy-start.1
  89.9 1.0 copy-start.2
  92.3 2.1 copy-start.1
  95.7 1.0 copy-start.2
  98.1 2.1 copy-start.1
  101.6 1.0 copy-start.2
  104.0 2.1 copy-start.1
  107.5 1.0 copy-start.2
  268.2 72.3 %copy-start.3 = (bf16[64,4096]{1,0:T(8,128)(2,1)S(1)}, bf16[64,4096]{1,0:T(8,128)(2,1)}, u32[]{:S(2)}) copy-start(bf16[64,4096]{1,0:T(8,128)(2,1)} %param.14) | copy-start | bytes 1572868
Sparse Core Ops, SparseCore 0:
  11.5 60.9 all-gather.4
  75.3 192.8 all-gather.6
where the time goes:
time: 358 us; the launch traced here: 352 us
  waiting for transfers between devices  180 us (50%)
  other arithmetic  80.4 us (22%)
  blocking collectives  35.9 us (10%)
  local copies, waits for them, and re-layouts  25.1 us (7%)
  matrix products  15.5 us (4%)
  between operations  14.2 us (4%)
    all_gather x1, waiting for transfers between devices, entering(): lax.all_gather(part.astype(kind), axis)  157 us
    select_n x32, other arithmetic, step(): return jax.tree.map(lambda a, b: jnp.where(reached, a, b), new, before)  70.8 us
    all_gather x1, blocking collectives, entering(): lax.all_gather(part.astype(kind), axis)  35.9 us
    all_gather x1, waiting for transfers between devices, per_device(): pairs = lax.all_gather(own_pairs, 'ctx', axis=1, tiled=True)  22.6 us
    unnamed x14, local copies, waits for them, and re-layouts  13.4 us
  transfers between devices with their start and end apart: 2, of which 2 were waited for; matrix products, arithmetic and copies ran while one was open for 11% of the time, Pallas kernels for 0%

commit v1 on v0

v1 whole, which is shorter than its diff:
```python
import functools
import math

import jax
import jax.numpy as jnp
from jax import lax
from jax.experimental import pallas as pl
from jax.experimental.pallas import tpu as pltpu
from jax.sharding import PartitionSpec as P

DH = 128
HQ = 32
KVH = 4
PLANE = 8
CHIPS = 4
NEG = -1e30
F32 = jnp.float32
BF16 = jnp.bfloat16


def dot(a, b, dims, precision=None):
    return lax.dot_general(
        a, b, (dims, ((), ())), precision=precision, preferred_element_type=F32
    )


def kernel(
    planes,
    q_lin,
    k_lin,
    v_lin,
    log_decay,
    pattern,
    q_soft,
    k_soft,
    v_soft,
    lin_out,
    soft_out,
    kv,
    ends,
    sums,
    gathered,
    totals,
    total_ends,
    prefix,
    outgoing,
    state,
    mixed,
    ell_ref,
    ell_rows,
    queries,
    top_ref,
    den_ref,
    acc_ref,
    kv_recv,
    col_send,
    in_send,
    sib_send,
    end_send,
    end_recv,
    sum_send,
    sum_recv,
    tot_send,
    tot_recv,
    tend_send,
    tend_recv,
    st_send,
    st_recv,
):
    tok = q_lin.shape[0]
    heads = log_decay.shape[1]
    per = heads // PLANE
    blocks = pattern.shape[1]
    width = tok // blocks
    kvw = k_soft.shape[1]
    group = HQ // KVH
    rows = group * tok
    me = lax.axis_index("ctx")
    z, j = me // PLANE, lax.rem(me, PLANE)
    chip, core = j // 2, lax.rem(j, 2)
    base = z * PLANE
    sibling = base + chip * 2 + (1 - core)

    def remote(src, dst, send, recv, device):
        return pltpu.make_async_remote_copy(
            src_ref=src,
            dst_ref=dst,
            send_sem=send,
            recv_sem=recv,
            device_id={"ctx": device},
            device_id_type=pl.DeviceIdType.MESH,
        )

    def span(s):
        return kv.at[s]

    def kv_copy(s, send, device):
        return remote(span(s), span(s), send, kv_recv.at[s], device)

    def other_chip(o):
        return lax.rem(chip + o, CHIPS)

    kv[me, :, :kvw] = k_soft[...]
    kv[me, :, kvw:] = v_soft[...]
    for p in range(PLANE):
        @pl.when(p > j)
        def _():
            kv[base + p] = jnp.zeros((tok, 2 * kvw), BF16)

    barrier = pltpu.get_barrier_semaphore()
    for o in range(1, PLANE):
        pl.semaphore_signal(
            barrier, inc=1, device_id={"ctx": base + lax.rem(j + o, PLANE)},
            device_id_type=pl.DeviceIdType.MESH,
        )
    for o in range(1, planes):
        pl.semaphore_signal(
            barrier, inc=1, device_id={"ctx": lax.rem(z + o, planes) * PLANE + j},
            device_id_type=pl.DeviceIdType.MESH,
        )
    pl.semaphore_wait(barrier, PLANE - 1 + planes - 1)

    def column(up, wait):
        copy = kv_copy(me, col_send.at[up], up * PLANE + j)
        copy.wait_send() if wait else copy.start()

    def column_all(wait):
        def body(up, c):
            column(up, wait)
            return c

        lax.fori_loop(z + 1, planes, body, 0)

    def own_row(wait):
        for o in range(1, CHIPS):
            k2 = other_chip(o)

            @pl.when(k2 > chip)
            def _():
                copy = kv_copy(me, in_send.at[z, o - 1], base + k2 * 2 + core)
                copy.wait_send() if wait else copy.start()

        @pl.when(core == 0)
        def _():
            copy = kv_copy(me, sib_send.at[z, 0], sibling)
            copy.wait_send() if wait else copy.start()

    def lower_row(r, wait):
        s = r * PLANE + j
        if not wait:
            kv_copy(s, col_send.at[r], me).wait_recv()
        for o in range(1, CHIPS):
            copy = kv_copy(s, in_send.at[r, o - 1], base + other_chip(o) * 2 + core)
            copy.wait_send() if wait else copy.start()
        copy = kv_copy(s, sib_send.at[r, 0], sibling)
        copy.wait_send() if wait else copy.start()

    def forward_row(r, wait):
        for o in range(1, CHIPS):
            s = r * PLANE + other_chip(o) * 2 + core
            if not wait:
                kv_copy(s, sib_send.at[r, o], sibling).wait_recv()
            copy = kv_copy(s, sib_send.at[r, o], sibling)
            copy.wait_send() if wait else copy.start()

    def forward_own(wait):
        for o in range(1, CHIPS):
            k2 = other_chip(o)

            @pl.when(k2 < chip)
            def _():
                s = base + k2 * 2 + core
                copy = kv_copy(s, sib_send.at[z, o], sibling)
                if not wait:
                    copy.wait_recv()
                copy.wait_send() if wait else copy.start()

    column_all(False)
    own_row(False)

    t_pos = lax.broadcasted_iota(jnp.int32, (tok, tok), 0)
    s_pos = lax.broadcasted_iota(jnp.int32, (tok, tok), 1)
    causal = s_pos <= t_pos
    tri = causal.astype(F32)
    high = lax.Precision.HIGHEST
    decay = log_decay[...]
    ell_ref[...] = dot(tri, decay, ((1,), (0,)), high)
    ell_rows[...] = dot(decay, tri, ((0,), (1,)), high)
    ends[j] = dot(decay, jnp.ones((tok, DH), F32), ((0,), (0,)), high)

    def end_copy(o):
        return remote(
            ends.at[j], ends.at[j], end_send.at[o], end_recv.at[j],
            base + lax.rem(j + o, PLANE),
        )

    for o in range(1, PLANE):
        end_copy(o).start()

    lane = lax.broadcasted_iota(jnp.int32, (tok, heads), 1)

    def column_of(h):
        return jnp.sum(jnp.where(lane == h, ell_ref[...], 0.0), axis=1, keepdims=True)

    def columns(h):
        return pl.ds(pl.multiple_of(h * DH, DH), DH)

    def sum_copy(o):
        g = lax.rem(j + o, PLANE)
        return remote(sums.at[g], gathered.at[j], sum_send.at[g], sum_recv.at[j], base + g)

    def summarize(i, c):
        g = lax.rem(j + i, PLANE)
        for u in range(per):
            h = g * per + u
            col = column_of(h)
            scaled = k_lin[:, columns(h)].astype(F32) * jnp.exp(col[tok - 1 : tok, :] - col)
            total = dot(scaled.astype(BF16), v_lin[:, columns(h)], ((0,), (0,)))
            sums[g, u * DH : (u + 1) * DH, :] = total.astype(BF16)

        @pl.when(i < PLANE)
        def _():
            sum_copy(i).start()

        return c

    lax.fori_loop(1, PLANE + 1, summarize, 0)
    gathered[j] = sums[j]

    def send_lower(r, c):
        lower_row(r, False)
        return c

    lax.fori_loop(0, z, send_lower, 0)

    t_blk, s_blk = t_pos // width, s_pos // width
    live = t_blk == s_blk
    for b in range(blocks):
        for a in range(b):
            live = live | (
                (t_blk == b) & (s_blk == a) & (pattern[b : b + 1, a : a + 1] == 1)
            )
    live = live & causal

    def within(g, c):
        for u in range(per):
            h = g * per + u
            cols = columns(h)
            scores = dot(q_lin[:, cols], k_lin[:, cols], ((1,), (1,)))
            diff = column_of(h) - ell_rows[pl.ds(h, 1), :]
            weight = jnp.where(live, scores * jnp.exp(jnp.where(live, diff, 0.0)), 0.0)
            mixed[:, cols] = dot(weight.astype(BF16), v_lin[:, cols], ((1,), (0,)))
        return c

    lax.fori_loop(0, PLANE, within, 0)

    for kh in range(KVH):
        for g in range(group):
            h = kh * group + g
            queries[kh, g * tok : (g + 1) * tok, :] = q_soft[:, h * DH : (h + 1) * DH]

    for o in range(1, PLANE):
        c = lax.rem(j + o, PLANE)
        remote(ends.at[c], ends.at[c], end_send.at[o], end_recv.at[c], me).wait_recv()
        remote(sums.at[c], gathered.at[c], sum_send.at[c], sum_recv.at[c], me).wait_recv()

    def scan(u, carry):
        at = pl.ds(pl.multiple_of(u * DH, DH), DH)
        run = jnp.zeros((DH, DH), F32)
        for c in range(PLANE):
            prefix[c, at, :] = run
            run = run * jnp.exp(ends[c, pl.ds(j * per + u, 1), :]) + gathered[c, at, :].astype(F32)
        totals[z, at, :] = run.astype(BF16)
        return carry

    lax.fori_loop(0, per, scan, 0)
    plane_end = ends[0]
    for c in range(1, PLANE):
        plane_end = plane_end + ends[c]
    total_ends[z] = plane_end

    def total_copies(up):
        device = up * PLANE + j
        return (
            remote(totals.at[z], totals.at[z], tot_send.at[up], tot_recv.at[z], device),
            remote(total_ends.at[z], total_ends.at[z], tend_send.at[up], tend_recv.at[z], device),
        )

    def send_totals(up, c):
        for copy in total_copies(up):
            copy.start()
        return c

    lax.fori_loop(z + 1, planes, send_totals, 0)

    factor = math.log2(math.e) / math.sqrt(DH)

    def fold(r, kh, first):
        at = pl.ds(pl.multiple_of(r * PLANE, PLANE), PLANE)
        keys = kv[at, :, kh * DH : (kh + 1) * DH].reshape(PLANE * tok, DH)
        values = kv[at, :, kvw + kh * DH : kvw + (kh + 1) * DH].reshape(PLANE * tok, DH)
        scores = dot(keys, queries[kh], ((1,), (1,)))
        if first:
            shape = (PLANE * tok, tok)
            key = lax.broadcasted_iota(jnp.int32, shape, 0)
            query = j * tok + lax.broadcasted_iota(jnp.int32, shape, 1)
            bias = jnp.where(key <= query, 0.0, NEG)
            scores = scores + jnp.concatenate([bias] * group, axis=1)
            top = jnp.max(scores, axis=0, keepdims=True)
        else:
            old = top_ref[kh]
            top = jnp.maximum(old, jnp.max(scores, axis=0, keepdims=True))
        probs = jnp.exp2(scores * factor - top * factor)
        den = jnp.sum(probs, axis=0, keepdims=True)
        acc = dot(values, probs.astype(BF16), ((0,), (0,)))
        if not first:
            shrink = jnp.exp2((old - top) * factor)
            den = den + den_ref[kh] * shrink
            acc = acc + acc_ref[kh] * shrink
        top_ref[kh] = top
        den_ref[kh] = den
        acc_ref[kh] = acc

    forward_own(False)
    for k2 in range(CHIPS):
        @pl.when((k2 < chip) | ((k2 == chip) & (core == 1)))
        def _():
            s = base + k2 * 2 + (1 - core)
            kv_copy(s, sib_send.at[z, 0], me).wait_recv()

    for kh in range(KVH):
        fold(z, kh, True)

    def take_totals(low, c):
        remote(totals.at[low], totals.at[low], tot_send.at[low], tot_recv.at[low], me).wait_recv()
        remote(
            total_ends.at[low], total_ends.at[low], tend_send.at[low], tend_recv.at[low], me
        ).wait_recv()
        return c

    lax.fori_loop(0, z, take_totals, 0)

    def enter(u, carry):
        at = pl.ds(pl.multiple_of(u * DH, DH), DH)
        row = pl.ds(j * per + u, 1)

        def add(low, run):
            return run * jnp.exp(total_ends[low, row, :]) + totals[low, at, :].astype(F32)

        start = lax.fori_loop(0, z, add, jnp.zeros((DH, DH), F32))
        past = jnp.zeros((1, DH), F32)
        for c in range(PLANE):
            outgoing[c, at, :] = (prefix[c, at, :] + start * jnp.exp(past)).astype(BF16)
            past = past + ends[c, row, :]
        return carry

    lax.fori_loop(0, per, enter, 0)

    def state_copy(o):
        c = lax.rem(j + o, PLANE)
        return remote(outgoing.at[c], state.at[j], st_send.at[c], st_recv.at[j], base + c)

    for o in range(1, PLANE):
        state_copy(o).start()
    state[j] = outgoing[j]

    @pl.when(z > 0)
    def _():
        forward_row(0, False)

    def lower(r, c):
        @pl.when(r + 1 < z)
        def _():
            forward_row(r + 1, False)

        for k2 in range(CHIPS):
            s = r * PLANE + k2 * 2 + (1 - core)
            kv_copy(s, sib_send.at[r, 0], me).wait_recv()
        for kh in range(KVH):
            fold(r, kh, False)
        return c

    lax.fori_loop(0, z, lower, 0)
    for kh in range(KVH):
        out = (acc_ref[kh] / den_ref[kh]).T
        for g in range(group):
            h = kh * group + g
            soft_out[:, h * DH : (h + 1) * DH] = out[g * tok : (g + 1) * tok, :].astype(BF16)

    for o in range(1, PLANE):
        c = lax.rem(j + o, PLANE)
        remote(outgoing.at[c], state.at[c], st_send.at[c], st_recv.at[c], me).wait_recv()

    def finish(g, c):
        for u in range(per):
            h = g * per + u
            cols = columns(h)
            inter = dot(q_lin[:, cols], state[g, u * DH : (u + 1) * DH, :], ((1,), (0,)))
            full = inter * jnp.exp(column_of(h)) + mixed[:, cols]
            mean = jnp.mean(full * full, axis=1, keepdims=True)
            lin_out[:, cols] = (full / jnp.sqrt(mean + 1e-6)).astype(BF16)
        return c

    lax.fori_loop(0, PLANE, finish, 0)

    column_all(True)
    own_row(True)
    forward_own(True)

    def drain_rows(r, c):
        lower_row(r, True)
        forward_row(r, True)
        return c

    lax.fori_loop(0, z, drain_rows, 0)

    def drain_totals(up, c):
        for copy in total_copies(up):
            copy.wait_send()
        return c

    lax.fori_loop(z + 1, planes, drain_totals, 0)
    for o in range(1, PLANE):
        end_copy(o).wait_send()
        sum_copy(o).wait_send()
        state_copy(o).wait_send()


def per_device(n, *args):
    q_lin, k_lin, v_lin, log_decay, pattern, q_soft, k_soft, v_soft = args
    tok, heads = log_decay.shape
    kvw = k_soft.shape[1]
    planes = n // PLANE
    share = heads // PLANE * DH
    rows = HQ // KVH * tok
    dma = pltpu.SemaphoreType.DMA
    vmem = pl.BlockSpec(memory_space=pltpu.VMEM)
    return pl.pallas_call(
        functools.partial(kernel, planes),
        out_shape=(
            jax.ShapeDtypeStruct(q_lin.shape, BF16),
            jax.ShapeDtypeStruct(q_soft.shape, BF16),
        ),
        in_specs=[vmem] * 8,
        out_specs=(vmem, vmem),
        scratch_shapes=[
            pltpu.VMEM((n, tok, 2 * kvw), BF16),
            pltpu.VMEM((PLANE, heads, DH), F32),
            pltpu.VMEM((PLANE, share, DH), BF16),
            pltpu.VMEM((PLANE, share, DH), BF16),
            pltpu.VMEM((planes, share, DH), BF16),
            pltpu.VMEM((planes, heads, DH), F32),
            pltpu.VMEM((PLANE, share, DH), F32),
            pltpu.VMEM((PLANE, share, DH), BF16),
            pltpu.VMEM((PLANE, share, DH), BF16),
            pltpu.VMEM((tok, heads * DH), F32),
            pltpu.VMEM((tok, heads), F32),
            pltpu.VMEM((heads, tok), F32),
            pltpu.VMEM((KVH, rows, DH), BF16),
            pltpu.VMEM((KVH, 1, rows), F32),
            pltpu.VMEM((KVH, 1, rows), F32),
            pltpu.VMEM((KVH, DH, rows), F32),
            dma((n,)),
            dma((planes,)),
            dma((planes, CHIPS - 1)),
            dma((planes, CHIPS)),
            dma((PLANE,)),
            dma((PLANE,)),
            dma((PLANE,)),
            dma((PLANE,)),
            dma((planes,)),
            dma((planes,)),
            dma((planes,)),
            dma((planes,)),
            dma((PLANE,)),
            dma((PLANE,)),
        ],
        compiler_params=pltpu.CompilerParams(
            collective_id=0, has_side_effects=True, vmem_limit_bytes=48 * 1024 * 1024
        ),
        name="both_layers",
    )(*args)


def solution(mesh):
    spec = P(("parts", "ctx"), None)
    return jax.shard_map(
        functools.partial(per_device, mesh.shape["ctx"]),
        mesh=mesh,
        in_specs=(spec,) * 8,
        out_specs=(spec, spec),
        check_vma=False,
    )
```

time: 358 us -> 63.5 us (0.18); the launches traced: 352 us -> 63 us
  waiting for transfers between devices: 180 us -> 0 us
  other arithmetic: 80.4 us -> 0 us
  Pallas kernels: 0 us -> 54.1 us
  blocking collectives: 35.9 us -> 0 us
  local copies, waits for them, and re-layouts: 25.1 us -> 8.23 us
  matrix products: 15.5 us -> 0 us
  between operations: 14.2 us -> 0.66 us
    all_gather x2 -> x0, waiting for transfers between devices: 179 us -> none  [the longest x1 157 us: entering(): lax.all_gather(part.astype(kind), axis)]
    select_n x32 -> x0, other arithmetic: 70.8 us -> none  [step(): return jax.tree.map(lambda a, b: jnp.where(reached, a, b), new, before)]
    pallas_call x0 -> x1, Pallas kernels: none -> 54.1 us  [per_device(): pl.pallas_call(functools.partial(kernel, planes), out_shape=(jax.ShapeDty...]
    all_gather x1 -> x0, blocking collectives: 35.9 us -> none  [entering(): lax.all_gather(part.astype(kind), axis)]
    dot_general x11 -> x0, matrix products: 15.5 us -> none  [the longest x4 5.52 us: fold_block(): jnp.einsum('kgts,skd->kgtd', probs.astype(jnp.bfloat16), block_values, pr...]
    slice x4 -> x0, local copies, waits for them, and re-layouts: 5.24 us -> none  [fold_block(): block_values = pairs[1].reshape(count, KVH, DH)]
    unnamed x14 -> x17, local copies, waits for them, and re-layouts: 13.4 us -> 8.23 us
    reduce_sum x4 -> x0, other arithmetic: 4.88 us -> none  [fold_block(): total = total * factor + jnp.sum(probs, axis=-1)]
  transfers between devices with their start and end apart: 2 -> 0, of which waited for: 2 -> 0; matrix products, arithmetic and copies ran while one was open for 11% -> 0% of each run, Pallas kernels for 0% -> 0%
where the time goes in v1:
time: 63.5 us; the launch traced here: 63 us
  Pallas kernels  54.1 us (85%)
  local copies, waits for them, and re-layouts  8.23 us (13%)
  between operations  0.66 us (1%)
    pallas_call x1, Pallas kernels, per_device(): pl.pallas_call(functools.partial(kernel, planes), out_shape=(jax.ShapeDty...  54.1 us
    unnamed x17, local copies, waits for them, and re-layouts  8.23 us

profile of v1, /device:TPU:31, one launch (start us, length us, event | category | flops | bytes accessed | tf_op | source)
XLA Modules:
  0.0 63.0 jit_solution(5294258754841568764)
XLA Ops:
  0.6 0.0 copy-start.6
  0.6 0.8 %copy.10.log_decay = f32[64,32]{1,0:T(8,128)S(1)} copy(f32[64,32]{0,1:T(8,128)} %param.11) | data formatting | bytes 16384 | tf_op args[3]
  1.4 0.0 copy-done.6
  1.4 0.0 copy-start
  1.5 1.0 %copy-done = bf16[64,4096]{1,0:T(8,128)(2,1)S(1)} copy-done((bf16[64,4096]{1,0:T(8,128)(2,1)S(1)}, bf16[64,4096]{1,0:T(8,128)(2,1)}, u32[]{:S(2)}) %copy-start) | copy-done | bytes 524312
  2.5 0.0 copy-start.1
  2.5 1.0 %copy-done.1 = bf16[64,4096]{1,0:T(8,128)(2,1)S(1)} copy-done((bf16[64,4096]{1,0:T(8,128)(2,1)S(1)}, bf16[64,4096]{1,0:T(8,128)(2,1)}, u32[]{:S(2)}) %copy-start.1) | copy-done | bytes 524312
  3.5 0.0 copy-start.2
  3.5 1.0 %copy-done.2 = bf16[64,4096]{1,0:T(8,128)(2,1)S(1)} copy-done((bf16[64,4096]{1,0:T(8,128)(2,1)S(1)}, bf16[64,4096]{1,0:T(8,128)(2,1)}, u32[]{:S(2)}) %copy-start.2) | copy-done | bytes 524312
  4.6 0.0 copy-start.3
  4.6 1.0 %copy-done.3 = bf16[64,4096]{1,0:T(8,128)(2,1)S(1)} copy-done((bf16[64,4096]{1,0:T(8,128)(2,1)S(1)}, bf16[64,4096]{1,0:T(8,128)(2,1)}, u32[]{:S(2)}) %copy-start.3) | copy-done | bytes 524312
  5.6 0.0 copy-start.4
  5.6 0.8 %copy-done.4 = bf16[64,512]{1,0:T(8,128)(2,1)S(1)} copy-done((bf16[64,512]{1,0:T(8,128)(2,1)S(1)}, bf16[64,512]{1,0:T(8,128)(2,1)}, u32[]{:S(2)}) %copy-start.4) | copy-done | bytes 65560
  6.5 0.0 copy-start.5
  6.5 0.8 %copy-done.5 = bf16[64,512]{1,0:T(8,128)(2,1)S(1)} copy-done((bf16[64,512]{1,0:T(8,128)(2,1)S(1)}, bf16[64,512]{1,0:T(8,128)(2,1)}, u32[]{:S(2)}) %copy-start.5) | copy-done | bytes 65560
  7.3 54.1 %both_layers.1 = (bf16[64,4096]{1,0:T(8,128)(2,1)S(1)}, bf16[64,4096]{1,0:T(8,128)(2,1)S(1)}) custom-call(bf16[64,4096]{1,0:T(8,128)(2,1)S(1)} %copy-done, bf16[64,4096]{1,0:T(8,128)(2,1)S(1)} %copy-done.1, bf16[64,4096]{1,0:T(8,128)(2,1)S(1)} %copy-done.2, f32[64,32]{1,0:T(8,128)S(1)} %copy.10.log_decay, s32[2,2]{1,0:T(2,128)S(1)} %copy-done.6, ...), custom_call_target="tpu_custom_call" | custom-call | tf_op jit(solution)/shard_map/both_layers/pallas_call | solution.py:438
  61.4 0.8 %copy.13 = bf16[64,4096]{1,0:T(8,128)(2,1)} copy(bf16[64,4096]{1,0:T(8,128)(2,1)S(1)} %get-tuple-element.4) | data formatting | bytes 1048576
  62.2 0.8 %copy.14 = bf16[64,4096]{1,0:T(8,128)(2,1)} copy(bf16[64,4096]{1,0:T(8,128)(2,1)S(1)} %get-tuple-element.5) | data formatting | bytes 1048576
Async XLA Ops:
  0.6 0.8 %copy-start.6 = (s32[2,2]{1,0:T(2,128)S(1)}, s32[2,2]{1,0:T(2,128)}, u32[]{:S(2)}) copy-start(s32[2,2]{1,0:T(2,128)} %pattern.1) | copy-start | bytes 52
  1.4 1.0 %copy-start = (bf16[64,4096]{1,0:T(8,128)(2,1)S(1)}, bf16[64,4096]{1,0:T(8,128)(2,1)}, u32[]{:S(2)}) copy-start(bf16[64,4096]{1,0:T(8,128)(2,1)} %q_lin.1) | copy-start | bytes 1572868
  2.5 1.0 %copy-start.1 = (bf16[64,4096]{1,0:T(8,128)(2,1)S(1)}, bf16[64,4096]{1,0:T(8,128)(2,1)}, u32[]{:S(2)}) copy-start(bf16[64,4096]{1,0:T(8,128)(2,1)} %k_lin.1) | copy-start | bytes 1572868
  3.5 1.0 %copy-start.2 = (bf16[64,4096]{1,0:T(8,128)(2,1)S(1)}, bf16[64,4096]{1,0:T(8,128)(2,1)}, u32[]{:S(2)}) copy-start(bf16[64,4096]{1,0:T(8,128)(2,1)} %v_lin.1) | copy-start | bytes 1572868
  4.6 1.0 %copy-start.3 = (bf16[64,4096]{1,0:T(8,128)(2,1)S(1)}, bf16[64,4096]{1,0:T(8,128)(2,1)}, u32[]{:S(2)}) copy-start(bf16[64,4096]{1,0:T(8,128)(2,1)} %q_soft.1) | copy-start | bytes 1572868
  5.6 0.8 %copy-start.4 = (bf16[64,512]{1,0:T(8,128)(2,1)S(1)}, bf16[64,512]{1,0:T(8,128)(2,1)}, u32[]{:S(2)}) copy-start(bf16[64,512]{1,0:T(8,128)(2,1)} %k_soft.1) | copy-start | bytes 196612
  6.5 0.8 %copy-start.5 = (bf16[64,512]{1,0:T(8,128)(2,1)S(1)}, bf16[64,512]{1,0:T(8,128)(2,1)}, u32[]{:S(2)}) copy-start(bf16[64,512]{1,0:T(8,128)(2,1)} %v_soft.1) | copy-start | bytes 196612

commit v2 on v1

--- a/solution.py
+++ b/solution.py
@@ -26,24 +26,33 @@
 
 def kernel(
     planes,
+    q_lin_hbm,
+    k_lin_hbm,
+    v_lin_hbm,
+    log_decay,
+    pattern,
+    q_soft_hbm,
+    k_soft_hbm,
+    v_soft_hbm,
+    lin_out,
+    soft_out,
     q_lin,
     k_lin,
     v_lin,
-    log_decay,
-    pattern,
     q_soft,
-    k_soft,
-    v_soft,
-    lin_out,
-    soft_out,
     kv,
     ends,
     sums,
+    theirs,
+    chip_sums,
     gathered,
-    totals,
-    total_ends,
     prefix,
+    plane_sum,
+    carry_in,
+    carry_out,
     outgoing,
+    entry,
+    handed,
     state,
     mixed,
     ell_ref,
@@ -52,27 +61,30 @@
     top_ref,
     den_ref,
     acc_ref,
+    load,
     kv_recv,
     col_send,
     in_send,
     sib_send,
     end_send,
     end_recv,
+    swap_send,
+    swap_recv,
     sum_send,
     sum_recv,
-    tot_send,
-    tot_recv,
-    tend_send,
-    tend_recv,
-    st_send,
-    st_recv,
+    up_send,
+    up_recv,
+    out_send,
+    out_recv,
+    hand_send,
+    hand_recv,
 ):
     tok = q_lin.shape[0]
-    heads = log_decay.shape[1]
+    heads = log_decay.shape[0]
     per = heads // PLANE
     blocks = pattern.shape[1]
     width = tok // blocks
-    kvw = k_soft.shape[1]
+    kvw = k_soft_hbm.shape[1]
     group = HQ // KVH
     rows = group * tok
     me = lax.axis_index("ctx")
@@ -100,8 +112,21 @@
     def other_chip(o):
         return lax.rem(chip + o, CHIPS)
 
-    kv[me, :, :kvw] = k_soft[...]
-    kv[me, :, kvw:] = v_soft[...]
+    loads = [
+        pltpu.make_async_copy(src, dst, load.at[i])
+        for i, (src, dst) in enumerate(
+            (
+                (k_soft_hbm, kv.at[me, :, pl.ds(0, kvw)]),
+                (v_soft_hbm, kv.at[me, :, pl.ds(kvw, kvw)]),
+                (k_lin_hbm, k_lin),
+                (v_lin_hbm, v_lin),
+                (q_lin_hbm, q_lin),
+                (q_soft_hbm, q_soft),
+            )
+        )
+    ]
+    for copy in loads:
+        copy.start()
     for p in range(PLANE):
         @pl.when(p > j)
         def _():
@@ -175,6 +200,8 @@
                     copy.wait_recv()
                 copy.wait_send() if wait else copy.start()
 
+    loads[0].wait()
+    loads[1].wait()
     column_all(False)
     own_row(False)
 
@@ -184,9 +211,9 @@
     tri = causal.astype(F32)
     high = lax.Precision.HIGHEST
     decay = log_decay[...]
-    ell_ref[...] = dot(tri, decay, ((1,), (0,)), high)
-    ell_rows[...] = dot(decay, tri, ((0,), (1,)), high)
-    ends[j] = dot(decay, jnp.ones((tok, DH), F32), ((0,), (0,)), high)
+    ell_ref[...] = dot(tri, decay, ((1,), (1,)), high)
+    ell_rows[...] = dot(decay, tri, ((1,), (1,)), high)
+    ends[j] = dot(decay, jnp.ones((tok, DH), F32), ((1,), (0,)), high)
 
     def end_copy(o):
         return remote(
@@ -205,27 +232,61 @@
     def columns(h):
         return pl.ds(pl.multiple_of(h * DH, DH), DH)
 
-    def sum_copy(o):
-        g = lax.rem(j + o, PLANE)
-        return remote(sums.at[g], gathered.at[j], sum_send.at[g], sum_recv.at[j], base + g)
-
-    def summarize(i, c):
-        g = lax.rem(j + i, PLANE)
-        for u in range(per):
-            h = g * per + u
-            col = column_of(h)
-            scaled = k_lin[:, columns(h)].astype(F32) * jnp.exp(col[tok - 1 : tok, :] - col)
-            total = dot(scaled.astype(BF16), v_lin[:, columns(h)], ((0,), (0,)))
-            sums[g, u * DH : (u + 1) * DH, :] = total.astype(BF16)
-
-        @pl.when(i < PLANE)
-        def _():
-            sum_copy(i).start()
-
-        return c
-
-    lax.fori_loop(1, PLANE + 1, summarize, 0)
-    gathered[j] = sums[j]
+    def head_of(u, c2, k2):
+        return (2 * k2 + c2) * per + u
+
+    def swap_copy(u):
+        return remote(
+            sums.at[u, 1 - core], theirs.at[u], swap_send.at[u], swap_recv.at[u], sibling
+        )
+
+    def summarize(u, carry):
+        for half in range(2):
+            c2 = (1 - core) if half == 0 else core
+            for k2 in range(CHIPS):
+                h = head_of(u, c2, k2)
+                col = column_of(h)
+                scaled = k_lin[:, columns(h)].astype(F32) * jnp.exp(col[tok - 1 : tok, :] - col)
+                total = dot(scaled.astype(BF16), v_lin[:, columns(h)], ((0,), (0,)))
+                sums[u, c2, k2] = total.astype(BF16)
+            if half == 0:
+                swap_copy(u).start()
+        return carry
+
+    loads[2].wait()
+    loads[3].wait()
+    lax.fori_loop(0, per, summarize, 0)
+
+    def end_wait(p):
+        remote(ends.at[p], ends.at[p], end_send.at[0], end_recv.at[p], me).wait_recv()
+
+    end_wait(chip * 2 + 1 - core)
+    first, second = chip * 2, chip * 2 + 1
+
+    def sum_copy(u, o):
+        k2 = other_chip(o)
+        return remote(
+            chip_sums.at[u, k2], gathered.at[u, chip], sum_send.at[u, k2],
+            sum_recv.at[u, chip], base + k2 * 2 + core,
+        )
+
+    def early(u, k2):
+        return jnp.where(core == 0, sums[u, core, k2], theirs[u, k2]).astype(F32)
+
+    def late(u, k2):
+        return jnp.where(core == 0, theirs[u, k2], sums[u, core, k2]).astype(F32)
+
+    def combine(u, carry):
+        swap_copy(u).wait_recv()
+        for k2 in range(CHIPS):
+            fade = jnp.exp(ends[second, pl.ds(head_of(u, core, k2), 1), :])
+            chip_sums[u, k2] = (early(u, k2) * fade + late(u, k2)).astype(BF16)
+        for o in range(1, CHIPS):
+            sum_copy(u, o).start()
+        gathered[u, chip] = chip_sums[u, chip]
+        return carry
+
+    lax.fori_loop(0, per, combine, 0)
 
     def send_lower(r, c):
         lower_row(r, False)
@@ -252,46 +313,89 @@
             mixed[:, cols] = dot(weight.astype(BF16), v_lin[:, cols], ((1,), (0,)))
         return c
 
+    loads[4].wait()
     lax.fori_loop(0, PLANE, within, 0)
 
+    loads[5].wait()
     for kh in range(KVH):
         for g in range(group):
             h = kh * group + g
             queries[kh, g * tok : (g + 1) * tok, :] = q_soft[:, h * DH : (h + 1) * DH]
 
     for o in range(1, PLANE):
-        c = lax.rem(j + o, PLANE)
-        remote(ends.at[c], ends.at[c], end_send.at[o], end_recv.at[c], me).wait_recv()
-        remote(sums.at[c], gathered.at[c], sum_send.at[c], sum_recv.at[c], me).wait_recv()
+        p = lax.rem(j + o, PLANE)
+
+        @pl.when(p != chip * 2 + 1 - core)
+        def _():
+            end_wait(p)
+
+    def chip_end(k2, row):
+        return ends[2 * k2, row, :] + ends[2 * k2 + 1, row, :]
 
     def scan(u, carry):
-        at = pl.ds(pl.multiple_of(u * DH, DH), DH)
+        for o in range(1, CHIPS):
+            k2 = other_chip(o)
+            remote(
+                chip_sums.at[u, k2], gathered.at[u, k2], sum_send.at[u, k2],
+                sum_recv.at[u, k2], me,
+            ).wait_recv()
+        row = pl.ds(j * per + u, 1)
         run = jnp.zeros((DH, DH), F32)
-        for c in range(PLANE):
-            prefix[c, at, :] = run
-            run = run * jnp.exp(ends[c, pl.ds(j * per + u, 1), :]) + gathered[c, at, :].astype(F32)
-        totals[z, at, :] = run.astype(BF16)
+        for k2 in range(CHIPS):
+            prefix[u, k2] = run
+            run = run * jnp.exp(chip_end(k2, row)) + gathered[u, k2].astype(F32)
+        plane_sum[u] = run
+
+        @pl.when(z == 0)
+        def _():
+            carry_in[u] = jnp.zeros((DH, DH), BF16)
+            carry_out[u] = run.astype(BF16)
+            if planes > 1:
+                up_copy(u).start()
+
         return carry
 
+    def up_copy(u):
+        return remote(
+            carry_out.at[u], carry_in.at[u], up_send.at[u], up_recv.at[u], me + PLANE
+        )
+
     lax.fori_loop(0, per, scan, 0)
-    plane_end = ends[0]
-    for c in range(1, PLANE):
-        plane_end = plane_end + ends[c]
-    total_ends[z] = plane_end
-
-    def total_copies(up):
-        device = up * PLANE + j
-        return (
-            remote(totals.at[z], totals.at[z], tot_send.at[up], tot_recv.at[z], device),
-            remote(total_ends.at[z], total_ends.at[z], tend_send.at[up], tend_recv.at[z], device),
-        )
-
-    def send_totals(up, c):
-        for copy in total_copies(up):
-            copy.start()
-        return c
-
-    lax.fori_loop(z + 1, planes, send_totals, 0)
+
+    def out_copy(u, o):
+        k2 = other_chip(o)
+        return remote(
+            outgoing.at[u, k2], entry.at[u, chip], out_send.at[u, k2],
+            out_recv.at[u, chip], base + k2 * 2 + core,
+        )
+
+    def enter(u, carry):
+        row = pl.ds(j * per + u, 1)
+
+        @pl.when(z > 0)
+        def _():
+            up_copy(u).wait_recv()
+
+        start = carry_in[u].astype(F32)
+
+        @pl.when((z > 0) & (z < planes - 1))
+        def _():
+            whole = chip_end(0, row)
+            for k2 in range(1, CHIPS):
+                whole = whole + chip_end(k2, row)
+            carry_out[u] = (start * jnp.exp(whole) + plane_sum[u]).astype(BF16)
+            up_copy(u).start()
+
+        past = jnp.zeros((1, DH), F32)
+        for k2 in range(CHIPS):
+            outgoing[u, k2] = (prefix[u, k2] + start * jnp.exp(past)).astype(BF16)
+            past = past + chip_end(k2, row)
+        for o in range(1, CHIPS):
+            out_copy(u, o).start()
+        entry[u, chip] = outgoing[u, chip]
+        return carry
+
+    lax.fori_loop(0, per, enter, 0)
 
     factor = math.log2(math.e) / math.sqrt(DH)
 
@@ -331,38 +435,25 @@
     for kh in range(KVH):
         fold(z, kh, True)
 
-    def take_totals(low, c):
-        remote(totals.at[low], totals.at[low], tot_send.at[low], tot_recv.at[low], me).wait_recv()
-        remote(
-            total_ends.at[low], total_ends.at[low], tend_send.at[low], tend_recv.at[low], me
-        ).wait_recv()
-        return c
-
-    lax.fori_loop(0, z, take_totals, 0)
-
-    def enter(u, carry):
-        at = pl.ds(pl.multiple_of(u * DH, DH), DH)
-        row = pl.ds(j * per + u, 1)
-
-        def add(low, run):
-            return run * jnp.exp(total_ends[low, row, :]) + totals[low, at, :].astype(F32)
-
-        start = lax.fori_loop(0, z, add, jnp.zeros((DH, DH), F32))
-        past = jnp.zeros((1, DH), F32)
-        for c in range(PLANE):
-            outgoing[c, at, :] = (prefix[c, at, :] + start * jnp.exp(past)).astype(BF16)
-            past = past + ends[c, row, :]
+    def hand_copy(u):
+        return remote(handed.at[u], state.at[u, core], hand_send.at[u], hand_recv.at[u], sibling)
+
+    def hand(u, carry):
+        for o in range(1, CHIPS):
+            k2 = other_chip(o)
+            remote(
+                outgoing.at[u, k2], entry.at[u, k2], out_send.at[u, k2], out_recv.at[u, k2], me
+            ).wait_recv()
+        for k2 in range(CHIPS):
+            fade = jnp.exp(ends[first, pl.ds(head_of(u, core, k2), 1), :])
+            chip_state = entry[u, k2].astype(F32)
+            later = chip_state * fade + early(u, k2)
+            state[u, core, k2] = jnp.where(core == 0, chip_state, later).astype(BF16)
+            handed[u, k2] = jnp.where(core == 0, later, chip_state).astype(BF16)
+        hand_copy(u).start()
         return carry
 
-    lax.fori_loop(0, per, enter, 0)
-
-    def state_copy(o):
-        c = lax.rem(j + o, PLANE)
-        return remote(outgoing.at[c], state.at[j], st_send.at[c], st_recv.at[j], base + c)
-
-    for o in range(1, PLANE):
-        state_copy(o).start()
-    state[j] = outgoing[j]
+    lax.fori_loop(0, per, hand, 0)
 
     @pl.when(z > 0)
     def _():
@@ -387,21 +478,26 @@
             h = kh * group + g
             soft_out[:, h * DH : (h + 1) * DH] = out[g * tok : (g + 1) * tok, :].astype(BF16)
 
-    for o in range(1, PLANE):
-        c = lax.rem(j + o, PLANE)
-        remote(outgoing.at[c], state.at[c], st_send.at[c], st_recv.at[c], me).wait_recv()
-
-    def finish(g, c):
-        for u in range(per):
-            h = g * per + u
-            cols = columns(h)
-            inter = dot(q_lin[:, cols], state[g, u * DH : (u + 1) * DH, :], ((1,), (0,)))
-            full = inter * jnp.exp(column_of(h)) + mixed[:, cols]
-            mean = jnp.mean(full * full, axis=1, keepdims=True)
-            lin_out[:, cols] = (full / jnp.sqrt(mean + 1e-6)).astype(BF16)
+    def await_hand(u, c):
+        remote(
+            handed.at[u], state.at[u, 1 - core], hand_send.at[u], hand_recv.at[u], me
+        ).wait_recv()
         return c
 
-    lax.fori_loop(0, PLANE, finish, 0)
+    lax.fori_loop(0, per, await_hand, 0)
+
+    def finish(u, c):
+        for c2 in range(2):
+            for k2 in range(CHIPS):
+                h = head_of(u, c2, k2)
+                cols = columns(h)
+                inter = dot(q_lin[:, cols], state[u, c2, k2], ((1,), (0,)))
+                full = inter * jnp.exp(column_of(h)) + mixed[:, cols]
+                mean = jnp.mean(full * full, axis=1, keepdims=True)
+                lin_out[:, cols] = (full / jnp.sqrt(mean + 1e-6)).astype(BF16)
+        return c
+
+    lax.fori_loop(0, per, finish, 0)
 
     column_all(True)
     own_row(True)
@@ -414,16 +510,23 @@
 
     lax.fori_loop(0, z, drain_rows, 0)
 
-    def drain_totals(up, c):
-        for copy in total_copies(up):
-            copy.wait_send()
-        return c
-
-    lax.fori_loop(z + 1, planes, drain_totals, 0)
     for o in range(1, PLANE):
         end_copy(o).wait_send()
-        sum_copy(o).wait_send()
-        state_copy(o).wait_send()
+
+    def drain(u, c):
+        swap_copy(u).wait_send()
+        hand_copy(u).wait_send()
+        for o in range(1, CHIPS):
+            sum_copy(u, o).wait_send()
+            out_copy(u, o).wait_send()
+
+        @pl.when(z < planes - 1)
+        def _():
+            up_copy(u).wait_send()
+
+        return c
+
+    lax.fori_loop(0, per, drain, 0)
 
 
 def per_device(n, *args):
@@ -431,28 +534,38 @@
     tok, heads = log_decay.shape
     kvw = k_soft.shape[1]
     planes = n // PLANE
-    share = heads // PLANE * DH
+    per = heads // PLANE
     rows = HQ // KVH * tok
     dma = pltpu.SemaphoreType.DMA
     vmem = pl.BlockSpec(memory_space=pltpu.VMEM)
+    hbm = pl.BlockSpec(memory_space=pltpu.HBM)
     return pl.pallas_call(
         functools.partial(kernel, planes),
         out_shape=(
             jax.ShapeDtypeStruct(q_lin.shape, BF16),
             jax.ShapeDtypeStruct(q_soft.shape, BF16),
         ),
-        in_specs=[vmem] * 8,
+        in_specs=[hbm] * 3 + [vmem] * 2 + [hbm] * 3,
         out_specs=(vmem, vmem),
         scratch_shapes=[
+            pltpu.VMEM(q_lin.shape, BF16),
+            pltpu.VMEM(q_lin.shape, BF16),
+            pltpu.VMEM(q_lin.shape, BF16),
+            pltpu.VMEM(q_soft.shape, BF16),
             pltpu.VMEM((n, tok, 2 * kvw), BF16),
             pltpu.VMEM((PLANE, heads, DH), F32),
-            pltpu.VMEM((PLANE, share, DH), BF16),
-            pltpu.VMEM((PLANE, share, DH), BF16),
-            pltpu.VMEM((planes, share, DH), BF16),
-            pltpu.VMEM((planes, heads, DH), F32),
-            pltpu.VMEM((PLANE, share, DH), F32),
-            pltpu.VMEM((PLANE, share, DH), BF16),
-            pltpu.VMEM((PLANE, share, DH), BF16),
+            pltpu.VMEM((per, 2, CHIPS, DH, DH), BF16),
+            pltpu.VMEM((per, CHIPS, DH, DH), BF16),
+            pltpu.VMEM((per, CHIPS, DH, DH), BF16),
+            pltpu.VMEM((per, CHIPS, DH, DH), BF16),
+            pltpu.VMEM((per, CHIPS, DH, DH), F32),
+            pltpu.VMEM((per, DH, DH), F32),
+            pltpu.VMEM((per, DH, DH), BF16),
+            pltpu.VMEM((per, DH, DH), BF16),
+            pltpu.VMEM((per, CHIPS, DH, DH), BF16),
+            pltpu.VMEM((per, CHIPS, DH, DH), BF16),
+            pltpu.VMEM((per, CHIPS, DH, DH), BF16),
+            pltpu.VMEM((per, 2, CHIPS, DH, DH), BF16),
             pltpu.VMEM((tok, heads * DH), F32),
             pltpu.VMEM((tok, heads), F32),
             pltpu.VMEM((heads, tok), F32),
@@ -460,26 +573,29 @@
             pltpu.VMEM((KVH, 1, rows), F32),
             pltpu.VMEM((KVH, 1, rows), F32),
             pltpu.VMEM((KVH, DH, rows), F32),
+            dma((6,)),
             dma((n,)),
             dma((planes,)),
             dma((planes, CHIPS - 1)),
             dma((planes, CHIPS)),
             dma((PLANE,)),
             dma((PLANE,)),
-            dma((PLANE,)),
-            dma((PLANE,)),
-            dma((planes,)),
-            dma((planes,)),
-            dma((planes,)),
-            dma((planes,)),
-            dma((PLANE,)),
-            dma((PLANE,)),
+            dma((per,)),
+            dma((per,)),
+            dma((per, CHIPS)),
+            dma((per, CHIPS)),
+            dma((per,)),
+            dma((per,)),
+            dma((per, CHIPS)),
+            dma((per, CHIPS)),
+            dma((per,)),
+            dma((per,)),
         ],
         compiler_params=pltpu.CompilerParams(
-            collective_id=0, has_side_effects=True, vmem_limit_bytes=48 * 1024 * 1024
+            collective_id=0, has_side_effects=True, vmem_limit_bytes=60 * 1024 * 1024
         ),
         name="both_layers",
-    )(*args)
+    )(q_lin, k_lin, v_lin, log_decay.T, pattern, q_soft, k_soft, v_soft)
 
 
 def solution(mesh):

time: 63.5 us -> 57.2 us (0.901)
  local copies, waits for them, and re-layouts: 8.23 us -> 2.72 us
    unnamed x17 -> x4, local copies, waits for them, and re-layouts: 8.23 us -> 2.72 us
where the time goes in v2:
time: 57.2 us; the launch traced here: 56.9 us
  Pallas kernels  53.5 us (94%)
  local copies, waits for them, and re-layouts  2.72 us (5%)
  between operations  0.65 us (1%)
    pallas_call x1, Pallas kernels, per_device(): pl.pallas_call(functools.partial(kernel, planes), out_shape=(jax.ShapeDty...  53.5 us
    unnamed x4, local copies, waits for them, and re-layouts  2.72 us

profile of v2, /device:TPU:31, one launch (start us, length us, event | category | flops | bytes accessed | tf_op | source)
XLA Modules:
  0.0 56.9 jit_solution(8356808500455403870)
XLA Ops:
  0.6 53.5 %both_layers.1 = (bf16[64,4096]{1,0:T(8,128)(2,1)}, bf16[64,4096]{1,0:T(8,128)(2,1)}) custom-call(bf16[64,4096]{1,0:T(8,128)(2,1)} %q_lin_hbm.1, bf16[64,4096]{1,0:T(8,128)(2,1)} %k_lin_hbm.1, bf16[64,4096]{1,0:T(8,128)(2,1)} %v_lin_hbm.1, f32[32,64]{1,0:T(8,128)} %bitcast.1, s32[2,2]{1,0:T(2,128)} %pattern.1, bf16[64,4096]{1,0:T(8,128)(2,1)} %q_soft_hbm.1, ...), custom_call_target="tpu_custom_call" | custom-call | tf_op jit(solution)/shard_map/both_layers/pallas_call | solution.py:542
  54.2 0.0 copy-start
  54.2 1.9 %copy.12 = bf16[64,4096]{1,0:T(8,128)(2,1)} copy(bf16[64,4096]{1,0:T(8,128)(2,1)} %get-tuple-element.4) | data formatting | bytes 1048576
  56.1 0.0 copy-done
  56.1 0.8 %copy.13 = bf16[64,4096]{1,0:T(8,128)(2,1)} copy(bf16[64,4096]{1,0:T(8,128)(2,1)S(1)} %copy-done) | data formatting | bytes 1048576
Async XLA Ops:
  54.2 1.9 %copy-start = (bf16[64,4096]{1,0:T(8,128)(2,1)S(1)}, bf16[64,4096]{1,0:T(8,128)(2,1)}, u32[]{:S(2)}) copy-start(bf16[64,4096]{1,0:T(8,128)(2,1)} %get-tuple-element.5) | copy-start | bytes 1572868

commit v3 on v2

--- a/solution.py
+++ b/solution.py
@@ -150,8 +150,8 @@
         copy.wait_send() if wait else copy.start()
 
     def column_all(wait):
-        def body(up, c):
-            column(up, wait)
+        def body(i, c):
+            column(planes + z - i, wait)
             return c
 
         lax.fori_loop(z + 1, planes, body, 0)
@@ -289,7 +289,7 @@
     lax.fori_loop(0, per, combine, 0)
 
     def send_lower(r, c):
-        lower_row(r, False)
+        lower_row(z - 1 - r, False)
         return c
 
     lax.fori_loop(0, z, send_lower, 0)
@@ -457,26 +457,7 @@
 
     @pl.when(z > 0)
     def _():
-        forward_row(0, False)
-
-    def lower(r, c):
-        @pl.when(r + 1 < z)
-        def _():
-            forward_row(r + 1, False)
-
-        for k2 in range(CHIPS):
-            s = r * PLANE + k2 * 2 + (1 - core)
-            kv_copy(s, sib_send.at[r, 0], me).wait_recv()
-        for kh in range(KVH):
-            fold(r, kh, False)
-        return c
-
-    lax.fori_loop(0, z, lower, 0)
-    for kh in range(KVH):
-        out = (acc_ref[kh] / den_ref[kh]).T
-        for g in range(group):
-            h = kh * group + g
-            soft_out[:, h * DH : (h + 1) * DH] = out[g * tok : (g + 1) * tok, :].astype(BF16)
+        forward_row(z - 1, False)
 
     def await_hand(u, c):
         remote(
@@ -498,6 +479,27 @@
         return c
 
     lax.fori_loop(0, per, finish, 0)
+
+    def lower(i, c):
+        r = z - 1 - i
+
+        @pl.when(r > 0)
+        def _():
+            forward_row(r - 1, False)
+
+        for k2 in range(CHIPS):
+            s = r * PLANE + k2 * 2 + (1 - core)
+            kv_copy(s, sib_send.at[r, 0], me).wait_recv()
+        for kh in range(KVH):
+            fold(r, kh, False)
+        return c
+
+    lax.fori_loop(0, z, lower, 0)
+    for kh in range(KVH):
+        out = (acc_ref[kh] / den_ref[kh]).T
+        for g in range(group):
+            h = kh * group + g
+            soft_out[:, h * DH : (h + 1) * DH] = out[g * tok : (g + 1) * tok, :].astype(BF16)
 
     column_all(True)
     own_row(True)

time: 57.2 us -> 56.6 us (0.990)
  no operation moved by 1% of the time
where the time goes in v3:
time: 56.6 us; the launch traced here: 56.3 us
  Pallas kernels  53 us (94%)
  local copies, waits for them, and re-layouts  2.72 us (5%)
  between operations  0.65 us (1%)
    pallas_call x1, Pallas kernels, per_device(): pl.pallas_call(functools.partial(kernel, planes), out_shape=(jax.ShapeDty...  53 us
    unnamed x4, local copies, waits for them, and re-layouts  2.72 us

profile of v3, /device:TPU:31, one launch (start us, length us, event | category | flops | bytes accessed | tf_op | source)
XLA Modules:
  0.0 56.3 jit_solution(17132738631083212739)
XLA Ops:
  0.6 53.0 %both_layers.1 = (bf16[64,4096]{1,0:T(8,128)(2,1)}, bf16[64,4096]{1,0:T(8,128)(2,1)}) custom-call(bf16[64,4096]{1,0:T(8,128)(2,1)} %q_lin_hbm.1, bf16[64,4096]{1,0:T(8,128)(2,1)} %k_lin_hbm.1, bf16[64,4096]{1,0:T(8,128)(2,1)} %v_lin_hbm.1, f32[32,64]{1,0:T(8,128)} %bitcast.1, s32[2,2]{1,0:T(2,128)} %pattern.1, bf16[64,4096]{1,0:T(8,128)(2,1)} %q_soft_hbm.1, ...), custom_call_target="tpu_custom_call" | custom-call | tf_op jit(solution)/shard_map/both_layers/pallas_call | solution.py:544
  53.6 0.0 copy-start
  53.6 1.9 %copy.12 = bf16[64,4096]{1,0:T(8,128)(2,1)} copy(bf16[64,4096]{1,0:T(8,128)(2,1)} %get-tuple-element.4) | data formatting | bytes 1048576
  55.5 0.0 copy-done
  55.5 0.8 %copy.13 = bf16[64,4096]{1,0:T(8,128)(2,1)} copy(bf16[64,4096]{1,0:T(8,128)(2,1)S(1)} %copy-done) | data formatting | bytes 1048576
Async XLA Ops:
  53.6 1.9 %copy-start = (bf16[64,4096]{1,0:T(8,128)(2,1)S(1)}, bf16[64,4096]{1,0:T(8,128)(2,1)}, u32[]{:S(2)}) copy-start(bf16[64,4096]{1,0:T(8,128)(2,1)} %get-tuple-element.5) | copy-start | bytes 1572868
